TPU v7x, 32 devices: a whole 2x2x4 slice. The times are simulated.
32 devices in a mesh: rep: 2 (over x), ep: 16 (over z, y, core).
Axes of the slice: x: 2, y: 2, z: 4, core: 2. Of those that a mesh axis runs over, the one named last changes fastest.
Arguments:
- tokens: bfloat16 [32, 7168], P(('rep', 'ep')), parts along dimension 0, may hold values from -3 to 3
- ffn_gain: float32 [7168], replicated, may hold values from 0.1 to 1.9
- gate_weight: bfloat16 [7168, 9216], P(None, 'ep'), may hold values from -0.0625 to 0.0625
- up_weight: bfloat16 [7168, 9216], P(None, 'ep'), may hold values from -0.0625 to 0.0625
- down_weight: bfloat16 [9216, 7168], P('ep'), may hold values from -0.0625 to 0.0625
- queries: bfloat16 [32, 128, 576], P(('rep', 'ep')), parts along dimension 0, may hold values from -14 to 14
- kv_cache: bfloat16 [32, 1024, 576], P(('rep', 'ep')), parts along dimension 0, may hold values from -6 to 6
- new_kv: bfloat16 [32, 576], P(('rep', 'ep')), parts along dimension 0, may hold values from -6 to 6
- lengths: int32 [32], P(('rep', 'ep')), parts along dimension 0, may hold values from 2 to 1024, as said below
- uv_weight: bfloat16 [128, 512, 128], P('ep'), may hold values from -0.25 to 0.25
- out_weight: bfloat16 [128, 128, 7168], P('ep'), may hold values from -0.125 to 0.125
- moe_gain: float32 [7168], replicated, may hold values from 0.1 to 1.9
- route_ids: int32 [32, 1], P(('rep', 'ep')), parts along dimension 0, may hold values from 0 to 1
- route_scores: float32 [32, 1], P(('rep', 'ep')), parts along dimension 0, may hold values from 0.05 to 1
- expert_gate: bfloat16 [16, 7168, 128], P('ep'), may hold values from -0.0625 to 0.0625
- expert_up: bfloat16 [16, 7168, 128], P('ep'), may hold values from -0.0625 to 0.0625
- expert_down: bfloat16 [16, 128, 7168], P('ep'), may hold values from -0.1875 to 0.1875
Outputs:
- after_attention: bfloat16 [32, 7168], P(('rep', 'ep')), parts along dimension 0
- layer_out: bfloat16 [32, 7168], P(('rep', 'ep')), parts along dimension 0
There are 2 independent parts, one for each index of `rep`. A program takes and returns all parts, laid end to end along the dimension named above; an argument that names none is the same for every part. Nothing has to cross between parts.
Inputs may be any that keep to these rules, and one draw needn't show every extreme that they name: `lengths`: every request has at least two cached positions; in every draw some request has exactly 1024.
All inputs are finite; a program needn't handle non-finite values.
Results may differ from a plain program's by a relative error of at most 0.008.
Values may be sent and summed in bfloat16 or wider, within the bound.
A program may use at most 128 MiB of HBM per device.

v0:
```python
import jax
import jax.numpy as jnp
from jax import lax
from jax.sharding import PartitionSpec as P

LAT = 512
ROPE = 64
HV = 128
GROUP = 8


def rms_norm(matrix, gain):
    values = matrix.astype(jnp.float32)
    mean_square = jnp.mean(values * values, axis=-1, keepdims=True)
    return values * lax.rsqrt(mean_square + 1e-06) * gain


def body(
    tokens,
    ffn_gain,
    gate_weight,
    up_weight,
    down_weight,
    queries,
    kv_cache,
    new_kv,
    lengths,
    uv_weight,
    out_weight,
    moe_gain,
    route_ids,
    route_scores,
    expert_gate,
    expert_up,
    expert_down,
):
    model_width = tokens.shape[1]
    normed = rms_norm(tokens, ffn_gain).astype(jnp.bfloat16)
    block_rows = lax.all_gather(normed, "ep", axis=0, tiled=True)
    gate_part = jnp.dot(block_rows, gate_weight, preferred_element_type=jnp.float32)
    up_part = jnp.dot(block_rows, up_weight, preferred_element_type=jnp.float32)
    ffn_hidden = (jax.nn.silu(gate_part) * up_part).astype(jnp.bfloat16)
    factor = (HV + ROPE) ** (-0.5)
    scores = (
        jnp.einsum("rhc,rtc->rht", queries, kv_cache, preferred_element_type=jnp.float32) * factor
    )
    positions = jnp.arange(kv_cache.shape[1], dtype=jnp.int32)
    usable = positions[None, None, :] < lengths[:, None, None]
    own_score = (
        jnp.einsum("rhc,rc->rh", queries, new_kv, preferred_element_type=jnp.float32) * factor
    )
    highest = jnp.maximum(jnp.max(jnp.where(usable, scores, -jnp.inf), axis=2), own_score)
    weights = jnp.where(usable, jnp.exp(scores - highest[:, :, None]), 0.0)
    own_weight = jnp.exp(own_score - highest)
    totals = jnp.sum(weights, axis=2) + own_weight
    probs_cache = (weights / totals[:, :, None]).astype(jnp.bfloat16)
    probs_own = (own_weight / totals).astype(jnp.bfloat16)
    context = jnp.einsum(
        "rht,rtl->rhl", probs_cache, kv_cache[:, :, :LAT], preferred_element_type=jnp.float32
    )
    context = context + probs_own.astype(jnp.float32)[:, :, None] * new_kv[:, None, :LAT].astype(
        jnp.float32
    )
    context = context.astype(jnp.bfloat16)
    head_context = lax.all_to_all(context, "ep", split_axis=1, concat_axis=0, tiled=True)
    head_out = jnp.einsum(
        "rhl,hlv->rhv", head_context, uv_weight, preferred_element_type=jnp.float32
    ).astype(jnp.bfloat16)
    flat_heads = head_out.reshape(head_out.shape[0], -1)
    flat_output = out_weight.reshape(-1, model_width)
    dense_part = jnp.dot(ffn_hidden, down_weight, preferred_element_type=jnp.float32)
    branch_sum = lax.psum_scatter(
        dense_part + jnp.dot(flat_heads, flat_output, preferred_element_type=jnp.float32),
        "ep",
        scatter_dimension=0,
        tiled=True,
    )
    after_attention = (tokens.astype(jnp.float32) + branch_sum).astype(jnp.bfloat16)
    moe_in = rms_norm(after_attention, moe_gain).astype(jnp.bfloat16)
    chosen_count = route_scores.shape[1]
    combine = (2.5 / chosen_count * route_scores).astype(jnp.bfloat16)
    expert_count = lax.axis_size("ep") // GROUP
    matches = route_ids[:, :, None] == jnp.arange(expert_count, dtype=jnp.int32)[None, None, :]
    table = jnp.sum(jnp.where(matches, combine.astype(jnp.float32)[:, :, None], 0.0), axis=1)
    gate_slice = expert_gate[0]
    up_slice = expert_up[0]
    down_slice = expert_down[0]
    rows_all, table_all = (
        lax.all_gather(moe_in, "ep", axis=0, tiled=True),
        lax.all_gather(table.astype(jnp.bfloat16), "ep", axis=0, tiled=True),
    )
    owned_expert = lax.axis_index("ep") // GROUP
    selector = (jnp.arange(expert_count, dtype=jnp.int32) == owned_expert).astype(jnp.float32)
    column = jnp.sum(table_all.astype(jnp.float32) * selector[None, :], axis=1)
    gate_part = jnp.dot(rows_all, gate_slice, preferred_element_type=jnp.float32)
    up_part = jnp.dot(rows_all, up_slice, preferred_element_type=jnp.float32)
    expert_part = jnp.dot(
        (jax.nn.silu(gate_part) * up_part).astype(jnp.bfloat16),
        down_slice,
        preferred_element_type=jnp.float32,
    )
    moe_out = lax.psum_scatter(expert_part * column[:, None], "ep", scatter_dimension=0, tiled=True)
    layer_out = (after_attention.astype(jnp.float32) + moe_out).astype(jnp.bfloat16)
    return (after_attention, layer_out)


def solution(mesh):
    in_specs = (
        P(("rep", "ep"), None),
        P(),
        P(None, "ep"),
        P(None, "ep"),
        P("ep", None),
        P(("rep", "ep"), None, None),
        P(("rep", "ep"), None, None),
        P(("rep", "ep"), None),
        P(("rep", "ep")),
        P("ep", None, None),
        P("ep", None, None),
        P(),
        P(("rep", "ep"), None),
        P(("rep", "ep"), None),
        P("ep", None, None),
        P("ep", None, None),
        P("ep", None, None),
    )
    out_specs = (P(("rep", "ep"), None), P(("rep", "ep"), None))
    return jax.shard_map(body, mesh=mesh, in_specs=in_specs, out_specs=out_specs, check_vma=False)
```

profile of v0, /device:TPU:0, one launch (start us, length us, event | category | flops | bytes accessed | tf_op | source)
XLA Modules:
  0.0 283.7 jit_solution(15959283466825422155)
XLA Ops:
  7.2 0.0 copy-start
  8.0 0.7 slice_convert_fusion
  8.8 1.8 select_reduce_fusion
  10.6 0.1 fusion.68
  10.8 0.2 fusion.23
  11.1 0.5 fusion.8
  11.6 0.2 copy.56
  11.8 0.5 broadcast.70
  12.3 1.4 reduce.6
  13.7 0.7 reshape.156
  14.4 7.4 %all-to-all-start = ((bf16[16,2,2048]{2,1,0:T(2,128)(2,1)}), bf16[16,2,2048]{2,1,0:T(2,128)(2,1)S(1)}, u32[]{:S(2)}, u32[]{:S(2)}) async-start(bf16[16,2,2048]{2,1,0:T(2,128)(2,1)} %reshape.156), calls=%async_computation | async-start | bytes 262144 | tf_op jit(solution)/shard_map/all_to_all | solution.py:65
  21.8 0.0 all-reduce.5.cloned.1.call-start
  21.9 0.7 multiply_reduce_fusion.1
  23.3 23.0 %all-gather = bf16[16,1,7168]{2,1,0:T(2,128)(2,1)S(1)} all-gather(bf16[1,1,7168]{2,1,0:T(2,128)(2,1)S(1)} %convert_bitcast_fusion.1), channel_id=1, replica_groups=mesh['rep'=2,'ep'=16] {'ep'}, dimensions={0}, use_global_device_ids=true | all-gather | bytes 243712 | tf_op jit(solution)/shard_map/all_gather | solution.py:39
  46.3 5.6 %fusion.33 = f32[16,576]{1,0:T(8,128)S(1)} fusion(bf16[7168,576]{0,1:T(8,128)(2,1)} %param.19, bf16[16,1,7168]{2,1,0:T(2,128)(2,1)S(1)} %all-gather), kind=kOutput, calls=%fused_computation.35 | convolution fusion | flops 132120576 | bytes 8523776 | tf_op jit(solution)/shard_map/dot_general | solution.py:40
  51.8 9.5 %fusion.22 = f32[16,7168]{1,0:T(8,128)S(1)} fusion(bf16[576,7168]{1,0:T(8,128)(2,1)} %param.21, bf16[7168,576]{0,1:T(8,128)(2,1)} %param.20, bf16[16,1,7168]{2,1,0:T(2,128)(2,1)S(1)} %all-gather, f32[16,576]{1,0:T(8,128)S(1)} %fusion.33), kind=kOutput, calls=%fused_computation.23 | convolution fusion | flops 264296448 | bytes 17240064 | tf_op jit(solution)/shard_map/dot_general | solution.py:71
  62.7 0.1 reshape.157
  62.9 7.4 %fusion = f32[16,7168]{1,0:T(8,128)} fusion(f32[16,7168]{1,0:T(8,128)S(1)} %fusion.22, bf16[8,128,7168]{2,1,0:T(8,128)(2,1)} %param.27, bf16[8,512,128]{2,1,0:T(8,128)(2,1)} %param.26, bf16[16,8,512]{2,1,0:T(8,128)(2,1)S(1)} %bitcast.96), kind=kOutput, calls=%fused_computation.2 | convolution fusion | flops 251789312 | bytes 16777216 | tf_op jit(solution)/shard_map/dot_general | solution.py:73
  70.3 0.0 all-reduce.5.cloned.1.call-update
  70.3 0.0 all-reduce.7.cloned.1.call-start
  70.4 17.3 %all-gather.2 = bf16[16,1,2]{2,1,0:T(2,128)(2,1)S(1)} all-gather(bf16[1,1,2]{2,1,0:T(2,128)(2,1)S(1)} %fusion.62), channel_id=1, replica_groups=mesh['rep'=2,'ep'=16] {'ep'}, dimensions={0}, use_global_device_ids=true | all-gather | bytes 68 | tf_op jit(solution)/shard_map/all_gather | solution.py:90
  87.7 0.1 copy.28
  87.8 0.6 dynamic-slice
  88.4 0.1 fusion.60
  88.5 69.1 %all-reduce.5.cloned.1.call-done = f32[16,7168]{1,0:T(8,128)} async-done(((f32[16,7168]{1,0:T(8,128)}), f32[16,7168]{1,0:T(8,128)}) %all-reduce.5.cloned.1.call-update) | async-done | bytes 458768
  157.6 2.2 multiply_reduce_fusion
  160.6 21.9 %all-gather.1 = bf16[16,1,7168]{2,1,0:T(2,128)(2,1)S(1)} all-gather(bf16[1,1,7168]{2,1,0:T(2,128)(2,1)S(1)} %convert_bitcast_fusion), channel_id=1, replica_groups=mesh['rep'=2,'ep'=16] {'ep'}, dimensions={0}, use_global_device_ids=true | all-gather | bytes 243712 | tf_op jit(solution)/shard_map/all_gather | solution.py:89
  182.5 1.9 fusion.4
  184.4 3.0 %convolution_multiply_fusion = f32[16,7168]{1,0:T(8,128)} fusion(bf16[1,128,7168]{2,1,0:T(8,128)(2,1)S(1)} %copy-done, bf16[1,7168,128]{2,1,0:T(8,128)(2,1)} %param.32, f32[16]{0:T(128)S(1)} %fusion.60, bf16[16,1,7168]{2,1,0:T(2,128)(2,1)S(1)} %all-gather.1, f32[16,128]{1,0:T(8,128)S(1)} %fusion.4), kind=kOutput, calls=%fused_computation | convolution fusion | flops 58847232 | bytes 4366400 | tf_op jit(solution)/shard_map/dot_general | solution.py:97
  187.4 0.0 all-reduce.7.cloned.1.call-update
  187.4 87.3 %all-reduce.7.cloned.1.call-done = f32[16,7168]{1,0:T(8,128)} async-done(((f32[16,7168]{1,0:T(8,128)}), f32[16,7168]{1,0:T(8,128)}) %all-reduce.7.cloned.1.call-update) | async-done | bytes 458768
  274.7 2.2 fusion.50
  (25 shorter events, 0.2 us)
Async XLA Ops:
  7.2 177.2 %copy-start = (bf16[1,128,7168]{2,1,0:T(8,128)(2,1)S(1)}, bf16[1,128,7168]{2,1,0:T(8,128)(2,1)}, u32[]{:S(2)}) copy-start(bf16[1,128,7168]{2,1,0:T(8,128)(2,1)} %param.33) | copy-start | bytes 5505028
  7.2 3.4 %copy-start.7 = (bf16[1,576]{1,0:T(2,128)(2,1)S(1)}, bf16[1,576]{1,0:T(2,128)(2,1)}, u32[]{:S(2)}) copy-start(bf16[1,576]{1,0:T(2,128)(2,1)} %param.24) | copy-start | bytes 3460
  7.2 3.4 %copy-start.2 = (bf16[1,128,576]{1,2,0:T(8,128)(2,1)S(1)}, bf16[1,128,576]{1,2,0:T(8,128)(2,1)}, u32[]{:S(2)}) copy-start(bf16[1,128,576]{1,2,0:T(8,128)(2,1)} %param.22) | copy-start | bytes 442372
  7.2 3.8 %copy-start.1 = (bf16[1,1024,576]{1,2,0:T(8,128)(2,1)S(1)}, bf16[1,1024,576]{1,2,0:T(8,128)(2,1)}, u32[]{:S(2)}) copy-start(bf16[1,1024,576]{1,2,0:T(8,128)(2,1)} %param.23) | copy-start | bytes 3538948
  11.0 10.8 %copy-start.3 = (bf16[1,7168]{1,0:T(2,128)(2,1)S(1)}, bf16[1,7168]{1,0:T(2,128)(2,1)}, u32[]{:S(2)}) copy-start(bf16[1,7168]{1,0:T(2,128)(2,1)} %param.17) | copy-start | bytes 43012
  11.0 12.2 %copy-start.5 = (f32[7168]{0:T(1024)S(1)}, f32[7168]{0:T(1024)}, u32[]{:S(2)}) copy-start(f32[7168]{0:T(1024)} %param.18) | copy-start | bytes 86020
  14.4 48.3 %all-to-all-start = ((bf16[16,2,2048]{2,1,0:T(2,128)(2,1)}), bf16[16,2,2048]{2,1,0:T(2,128)(2,1)S(1)}, u32[]{:S(2)}, u32[]{:S(2)}) async-start(bf16[16,2,2048]{2,1,0:T(2,128)(2,1)} %reshape.156), calls=%async_computation | async-start | bytes 262144 | tf_op jit(solution)/shard_map/all_to_all | solution.py:65
  21.8 135.8 %all-reduce.5.cloned.1.call-start = ((), (), s32[]{:S(2)}) async-start(), calls=%async_computation.1 | async-start | bytes 917504
  62.8 25.0 %copy-start.8 = (u32[32]{0:T(128)S(1)}, u32[32]{0:T(128)}, u32[]{:S(2)}) copy-start(u32[32]{0:T(128)} %constant.58) | copy-start | bytes 388
  62.8 97.7 %copy-start.6 = (f32[7168]{0:T(1024)S(1)}, f32[7168]{0:T(1024)}, u32[]{:S(2)}) copy-start(f32[7168]{0:T(1024)} %param.28) | copy-start | bytes 86020
  70.3 204.4 %all-reduce.7.cloned.1.call-start = ((), (), s32[]{:S(2)}) async-start(), calls=%async_computation.2 | async-start | bytes 917504
  159.8 114.9 %copy-start.4 = (bf16[1,7168]{1,0:T(2,128)(2,1)}, bf16[1,7168]{1,0:T(2,128)(2,1)S(1)}, u32[]{:S(2)}) copy-start(bf16[1,7168]{1,0:T(2,128)(2,1)S(1)} %get-tuple-element.3) | copy-start | bytes 43012
Sparse Core Ops, SparseCore 0:
  70.4 87.1 all-reduce.4
  187.6 87.0 all-reduce.6
where the time goes:
time: 284 us
  waiting for transfers between devices  156 us (55%)
  blocking collectives  62.3 us (22%)
  matrix products  29.9 us (11%)
  between operations  17.8 us (6%)
  other arithmetic  7.65 us (3%)
  starting transfers between devices  7.47 us (3%)
    unnamed x4, waiting for transfers between devices  156 us
    all_gather x1, blocking collectives, body(): block_rows = lax.all_gather(normed, 'ep', axis=0, tiled=True)  23 us
    all_gather x1, blocking collectives, body(): lax.all_gather(moe_in, 'ep', axis=0, tiled=True)  21.9 us
    all_gather x1, blocking collectives, body(): lax.all_gather(table.astype(jnp.bfloat16), 'ep', axis=0, tiled=True)  17.3 us
    dot_general x1, matrix products, body(): jnp.dot(ffn_hidden, down_weight, preferred_element_type=jnp.float32)  9.53 us
    dot_general x1, matrix products, body(): jnp.dot(flat_heads, flat_output, preferred_element_type=jnp.float32)  7.41 us
    all_to_all x1, starting transfers between devices, body(): lax.all_to_all(context, 'ep', split_axis=1, concat_axis=0, tiled=True)  7.38 us
  transfers between devices with their start and end apart: 3, of which 2 were waited for; matrix products, arithmetic and copies ran while one was open for 6% of the time, Pallas kernels for 0%

commit v1 on v0

v1 whole, which is shorter than its diff:
```python
import functools

import jax
import jax.numpy as jnp
from jax import lax
from jax.experimental import pallas as pl
from jax.experimental.pallas import tpu as pltpu
from jax.sharding import PartitionSpec as P

LAT = 512
ROPE = 64
HV = 128
GROUP = 8
W = 512
F32 = jnp.float32
BF16 = jnp.bfloat16
MESH = pl.DeviceIdType.MESH


def dot(a, b):
    return jnp.dot(a, b, preferred_element_type=F32)


def silu(v):
    return v / (1.0 + jnp.exp(-v))


class Exchange:
    def __init__(self, n, me, src, dst, send_sem, recv_sem):
        self.n, self.me, self.src, self.dst = n, me, src, dst
        self.send_sem, self.recv_sem = send_sem, recv_sem

    def copy(self, d, slot):
        peer = lax.rem(self.me + d, self.n)
        return pltpu.make_async_remote_copy(
            src_ref=self.src(peer),
            dst_ref=self.dst.at[slot],
            send_sem=self.send_sem.at[d],
            recv_sem=self.recv_sem.at[d],
            device_id={"ep": peer},
            device_id_type=MESH,
        )

    def start(self):
        @pl.loop(1, self.n)
        def _(d):
            self.copy(d, self.me).start()

    def wait_recv(self):
        @pl.loop(1, self.n)
        def _(d):
            self.copy(d, lax.rem(self.me - d + self.n, self.n)).wait_recv()

    def wait_send(self):
        @pl.loop(1, self.n)
        def _(d):
            self.copy(d, self.me).wait_send()


def kernel(
    n, hpd, tok_ref, gain_ref, nkv_ref, len_ref, gain2_ref, ids_ref, score_ref,
    q_hbm, kv_hbm, gate_hbm, up_hbm, uv_hbm, out_hbm, down_hbm, eg_hbm, eu_hbm, ed_hbm,
    after_ref, layer_ref,
    q, kv, gate, up, uv, out, down, eg, eu, ed,
    row_f32, gain_rows, send1, recv1, ctx_send, ctx_recv, rs1_send, rs1_recv,
    send2, recv2, rs2_send, rs2_recv, wide, lhs, flat,
    load_sem, ssem, rsem,
):
    width = tok_ref.shape[1]
    chunks = width // W
    me = lax.axis_index("ep")
    barrier = pltpu.get_barrier_semaphore()

    @pl.loop(1, n)
    def _(d):
        pl.semaphore_signal(
            barrier, inc=1, device_id={"ep": lax.rem(me + d, n)}, device_id_type=MESH
        )

    loads = [
        pltpu.make_async_copy(src, dst, load_sem.at[i])
        for i, (src, dst) in enumerate(
            [(q_hbm, q), (kv_hbm, kv), (gate_hbm, gate), (up_hbm, up), (uv_hbm, uv),
             (out_hbm, out), (down_hbm, down), (eg_hbm, eg), (eu_hbm, eu), (ed_hbm, ed)]
        )
    ]
    for load in loads:
        load.start()
    (q_in, kv_in, gate_in, up_in, uv_in, out_in, down_in, eg_in, eu_in, ed_in) = loads

    def fold(src, dst):
        dst[...] = jnp.zeros_like(dst)
        for c in range(chunks):
            dst[c : c + 1, :] = src[0:1, c * W : (c + 1) * W].astype(F32)

    def norm(values, gain):
        squares = jnp.sum(jnp.sum(values * values, axis=1, keepdims=True), axis=0, keepdims=True)
        return values * lax.rsqrt(squares / width + 1e-06) * gain

    def unfold_rows(buffer):
        wide[...] = buffer[...].astype(F32)
        for c in range(chunks):
            lhs[c] = wide[:, c, :].astype(BF16)

    def total(buffer):
        def step(i, acc):
            return acc + buffer[i].astype(F32)

        return lax.fori_loop(0, n, step, jnp.zeros((16, W), F32), unroll=4)

    rows = lax.broadcasted_iota(jnp.int32, (16, W), 0)
    lanes = lax.broadcasted_iota(jnp.int32, (16, W), 1)

    fold(tok_ref, row_f32)
    fold(gain_ref, gain_rows)
    send1[...] = norm(row_f32[...], gain_rows[...]).astype(BF16)
    gather1 = Exchange(n, me, lambda peer: send1, recv1, ssem.at[0], rsem.at[0])
    recv1[me] = send1[...]
    pl.semaphore_wait(barrier, n - 1)
    gather1.start()

    q_in.wait()
    kv_in.wait()
    factor = (HV + ROPE) ** (-0.5)
    keys = kv[...]
    queries = q[...]
    scores = (
        lax.dot_general(queries, keys, (((1,), (1,)), ((), ())), preferred_element_type=F32)
        * factor
    )
    fresh = nkv_ref[...].astype(F32)
    own = jnp.sum(queries.astype(F32) * fresh, axis=1, keepdims=True) * factor
    usable = lax.broadcasted_iota(jnp.int32, scores.shape, 1) < len_ref[...]
    highest = jnp.maximum(
        jnp.max(jnp.where(usable, scores, -jnp.inf), axis=1, keepdims=True), own
    )
    weights = jnp.where(usable, jnp.exp(scores - highest), 0.0)
    own_weight = jnp.exp(own - highest)
    totals = jnp.sum(weights, axis=1, keepdims=True) + own_weight
    probs = (weights / totals).astype(BF16)
    probs_own = (own_weight / totals).astype(BF16).astype(F32)
    context = dot(probs, kv[:, :LAT]) + probs_own * fresh[:, :LAT]
    ctx_send[...] = context.astype(BF16).astype(F32).reshape(ctx_send.shape)
    ctx_recv[me] = ctx_send[me]
    spread = Exchange(n, me, lambda peer: ctx_send.at[peer], ctx_recv, ssem.at[1], rsem.at[1])
    spread.start()

    gather1.wait_recv()
    unfold_rows(recv1)
    gate_in.wait()
    up_in.wait()
    gate_part = jnp.zeros((n, gate.shape[1]), F32)
    up_part = jnp.zeros((n, up.shape[1]), F32)
    for c in range(chunks):
        part = slice(c * W, (c + 1) * W)
        gate_part += dot(lhs[c], gate[part, :])
        up_part += dot(lhs[c], up[part, :])
    hidden = (silu(gate_part) * up_part).astype(BF16)

    spread.wait_recv()
    uv_in.wait()
    for h in range(hpd):
        flat[:, h * HV : (h + 1) * HV] = dot(ctx_recv[:, h, :].astype(BF16), uv[h]).astype(BF16)
    out_in.wait()
    down_in.wait()
    heads = flat[...]
    for c in range(chunks):
        part = slice(c * W, (c + 1) * W)
        wide[:, c, :] = dot(hidden, down[:, part]) + dot(heads, out[:, part])
    rs1_send[...] = wide[...].astype(BF16)
    rs1_recv[me] = rs1_send[me]
    sum1 = Exchange(n, me, lambda peer: rs1_send.at[peer], rs1_recv, ssem.at[2], rsem.at[2])
    sum1.start()
    fold(gain2_ref, gain_rows)
    combine = (2.5 / ids_ref.shape[1] * score_ref[...]).astype(BF16).astype(F32)
    table = jnp.zeros((16, W), F32)
    for k in range(ids_ref.shape[1]):
        table += jnp.where(lanes == ids_ref[0:1, k : k + 1], combine[0:1, k : k + 1], 0.0)
    sum1.wait_recv()
    after = jnp.where(rows < chunks, row_f32[...] + total(rs1_recv), 0.0).astype(BF16).astype(F32)
    for c in range(chunks):
        after_ref[0:1, c * W : (c + 1) * W] = after[c : c + 1, :].astype(BF16)
    row_f32[...] = after

    moe_in = norm(after, gain_rows[...])
    send2[...] = jnp.where(rows == chunks, table, moe_in).astype(BF16)
    recv2[me] = send2[...]
    gather2 = Exchange(n, me, lambda peer: send2, recv2, ssem.at[3], rsem.at[3])
    gather2.start()
    eg_in.wait()
    eu_in.wait()
    ed_in.wait()
    gather2.wait_recv()
    unfold_rows(recv2)
    columns = wide[:, chunks, :]
    mine = lax.broadcasted_iota(jnp.int32, columns.shape, 1) == me // GROUP
    column = jnp.sum(jnp.where(mine, columns, 0.0), axis=1, keepdims=True)
    gate_part = jnp.zeros((n, eg.shape[1]), F32)
    up_part = jnp.zeros((n, eu.shape[1]), F32)
    for c in range(chunks):
        part = slice(c * W, (c + 1) * W)
        gate_part += dot(lhs[c], eg[part, :])
        up_part += dot(lhs[c], eu[part, :])
    expert_hidden = (silu(gate_part) * up_part).astype(BF16)
    for c in range(chunks):
        wide[:, c, :] = dot(expert_hidden, ed[:, c * W : (c + 1) * W]) * column
    rs2_send[...] = wide[...].astype(BF16)
    rs2_recv[me] = rs2_send[me]
    sum2 = Exchange(n, me, lambda peer: rs2_send.at[peer], rs2_recv, ssem.at[4], rsem.at[4])
    sum2.start()
    gather1.wait_send()
    spread.wait_send()
    sum1.wait_send()
    gather2.wait_send()
    sum2.wait_recv()
    layer = row_f32[...] + total(rs2_recv)
    for c in range(chunks):
        layer_ref[0:1, c * W : (c + 1) * W] = layer[c : c + 1, :].astype(BF16)
    sum2.wait_send()


def body(
    tokens, ffn_gain, gate_weight, up_weight, down_weight, queries, kv_cache, new_kv, lengths,
    uv_weight, out_weight, moe_gain, route_ids, route_scores, expert_gate, expert_up, expert_down,
):
    n = lax.axis_size("ep")
    width = tokens.shape[1]
    hpd = uv_weight.shape[0]
    chunks = width // W
    assert tokens.shape[0] == 1 and width % W == 0 and chunks < 16
    big = (
        queries[0], kv_cache[0], gate_weight, up_weight, uv_weight,
        out_weight.reshape(-1, width), down_weight,
        expert_gate[0], expert_up[0], expert_down[0],
    )
    vmem = pl.BlockSpec(memory_space=pltpu.VMEM)
    slots = pltpu.VMEM((n, 16, W), BF16)
    return pl.pallas_call(
        functools.partial(kernel, n, hpd),
        out_shape=[jax.ShapeDtypeStruct((1, width), BF16)] * 2,
        in_specs=[vmem] * 7 + [pl.BlockSpec(memory_space=pl.ANY)] * len(big),
        out_specs=[vmem] * 2,
        scratch_shapes=[pltpu.VMEM(x.shape, x.dtype) for x in big]
        + [
            pltpu.VMEM((16, W), F32),
            pltpu.VMEM((16, W), F32),
            pltpu.VMEM((16, W), BF16),
            slots,
            pltpu.VMEM((n, hpd, LAT), F32),
            pltpu.VMEM((n, hpd, LAT), F32),
            slots,
            slots,
            pltpu.VMEM((16, W), BF16),
            slots,
            slots,
            slots,
            pltpu.VMEM((n, 16, W), F32),
            pltpu.VMEM((chunks, n, W), BF16),
            pltpu.VMEM((n, hpd * HV), BF16),
            pltpu.SemaphoreType.DMA((len(big),)),
            pltpu.SemaphoreType.DMA((5, n)),
            pltpu.SemaphoreType.DMA((5, n)),
        ],
        compiler_params=pltpu.CompilerParams(
            collective_id=0, has_side_effects=True, vmem_limit_bytes=60 * 1024 * 1024
        ),
    )(
        tokens, ffn_gain.reshape(1, width), new_kv, lengths.reshape(1, 1),
        moe_gain.reshape(1, width), route_ids, route_scores, *big,
    )


def solution(mesh):
    in_specs = (
        P(("rep", "ep"), None),
        P(),
        P(None, "ep"),
        P(None, "ep"),
        P("ep", None),
        P(("rep", "ep"), None, None),
        P(("rep", "ep"), None, None),
        P(("rep", "ep"), None),
        P(("rep", "ep")),
        P("ep", None, None),
        P("ep", None, None),
        P(),
        P(("rep", "ep"), None),
        P(("rep", "ep"), None),
        P("ep", None, None),
        P("ep", None, None),
        P("ep", None, None),
    )
    out_specs = (P(("rep", "ep"), None), P(("rep", "ep"), None))
    return jax.shard_map(body, mesh=mesh, in_specs=in_specs, out_specs=out_specs, check_vma=False)
```

time: 284 us -> 82.7 us (0.29)
  waiting for transfers between devices: 156 us -> 0 us
  blocking collectives: 62.3 us -> 0 us
  Pallas kernels: 0 us -> 47 us
  matrix products: 29.9 us -> 0 us
  local copies, waits for them, and re-layouts: 2.32 us -> 31.7 us
  between operations: 17.8 us -> 2.58 us
  other arithmetic: 7.65 us -> 0 us
  starting transfers between devices: 7.47 us -> 0 us
    unnamed x4 -> x0, waiting for transfers between devices: 156 us -> none
    all_gather x3 -> x0, blocking collectives: 62.3 us -> none  [the longest x1 23 us: body(): block_rows = lax.all_gather(normed, 'ep', axis=0, tiled=True)]
    pallas_call x0 -> x1, Pallas kernels: none -> 47 us  [body(): pl.pallas_call(functools.partial(kernel, n, hpd), out_shape=[jax.ShapeDty...]
    dot_general x8 -> x0, matrix products: 29.9 us -> none  [the longest x1 9.53 us: body(): jnp.dot(ffn_hidden, down_weight, preferred_element_type=jnp.float32)]
    unnamed x23 -> x6, local copies, waits for them, and re-layouts: 2.03 us -> 31.7 us
    all_to_all x1 -> x0, starting transfers between devices: 7.38 us -> none  [body(): lax.all_to_all(context, 'ep', split_axis=1, concat_axis=0, tiled=True)]
    reduce_sum x4 -> x0, other arithmetic: 3.2 us -> none  [the longest x2 2.87 us: rms_norm(): mean_square = jnp.mean(values * values, axis=-1, keepdims=True)]
    convert_element_type x4 -> x0, other arithmetic: 2.95 us -> none  [the longest x1 2.19 us: body(): (after_attention.astype(jnp.float32) + moe_out).astype(jnp.bfloat16)]
  transfers between devices with their start and end apart: 3 -> 0, of which waited for: 2 -> 0; matrix products, arithmetic and copies ran while one was open for 6% -> 0% of each run, Pallas kernels for 0% -> 0%
where the time goes in v1:
time: 82.7 us; the launch traced here: 81.3 us
  Pallas kernels  47 us (57%)
  local copies, waits for them, and re-layouts  31.7 us (38%)
  between operations  2.58 us (3%)
    pallas_call x1, Pallas kernels, body(): pl.pallas_call(functools.partial(kernel, n, hpd), out_shape=[jax.ShapeDty...  47 us
    unnamed x6, local copies, waits for them, and re-layouts  31.7 us

profile of v1, /device:TPU:0, one launch (start us, length us, event | category | flops | bytes accessed | tf_op | source)
XLA Modules:
  0.0 81.3 jit_solution(13826128108742401888)
XLA Ops:
  2.6 1.7 %copy.19 = bf16[1,128,576]{2,1,0:T(8,128)(2,1)} copy(bf16[1,128,576]{1,2,0:T(8,128)(2,1)} %param.22) | data formatting | bytes 294912 | tf_op args[5]
  4.3 2.4 %copy.20 = bf16[1,1024,576]{2,1,0:T(8,128)(2,1)} copy(bf16[1,1024,576]{1,2,0:T(8,128)(2,1)} %param.23) | data formatting | bytes 2359296 | tf_op args[6]
  6.7 12.4 %copy.21.gate_hbm = bf16[7168,576]{1,0:T(8,128)(2,1)} copy(bf16[7168,576]{0,1:T(8,128)(2,1)} %param.19) | data formatting | bytes 16515072 | tf_op args[2]
  19.1 12.4 %copy.22.up_hbm = bf16[7168,576]{1,0:T(8,128)(2,1)} copy(bf16[7168,576]{0,1:T(8,128)(2,1)} %param.20) | data formatting | bytes 16515072 | tf_op args[3]
  31.5 47.0 %shard_map.176 = (bf16[1,7168]{1,0:T(2,128)(2,1)}, bf16[1,7168]{1,0:T(2,128)(2,1)}) custom-call(bf16[1,7168]{1,0:T(2,128)(2,1)} %tok_ref.1, f32[1,7168]{1,0:T(1,128)} %bitcast.16, bf16[1,576]{1,0:T(2,128)(2,1)} %nkv_ref.1, s32[1,1]{1,0:T(1,128)} %bitcast.9.len_ref, f32[1,7168]{1,0:T(1,128)} %bitcast.17, s32[1,1]{1,0:T(1,128)S(6)} %copy.26.ids_ref, ...), custom_call_target="tpu_custom_call" | custom-call | tf_op jit(solution)/shard_map/pallas_call | solution.py:238
  78.5 1.4 %copy.28 = bf16[1,7168]{1,0:T(2,128)(2,1)} copy(bf16[1,7168]{1,0:T(2,128)(2,1)} %get-tuple-element.4) | data formatting | bytes 28672
  79.9 1.4 %copy.29 = bf16[1,7168]{1,0:T(2,128)(2,1)} copy(bf16[1,7168]{1,0:T(2,128)(2,1)} %get-tuple-element.5) | data formatting | bytes 28672

commit v2 on v1

v2 whole, which is shorter than its diff:
```python
import functools

import jax
import jax.numpy as jnp
from jax import lax
from jax.experimental import pallas as pl
from jax.experimental.pallas import tpu as pltpu
from jax.sharding import PartitionSpec as P

LAT = 512
ROPE = 64
HV = 128
GROUP = 8
W = 256
F32 = jnp.float32
BF16 = jnp.bfloat16
MESH = pl.DeviceIdType.MESH


def dot(a, b):
    return jnp.dot(a, b, preferred_element_type=F32)


def dot_nt(a, b):
    return lax.dot_general(a, b, (((1,), (1,)), ((), ())), preferred_element_type=F32)


def silu(v):
    return v / (1.0 + jnp.exp(-v))


class Exchange:
    def __init__(self, n, me, src, dst, send_sem, recv_sem):
        self.n, self.me, self.src, self.dst = n, me, src, dst
        self.send_sem, self.recv_sem = send_sem, recv_sem

    def copy(self, d, slot):
        peer = lax.rem(self.me + d, self.n)
        return pltpu.make_async_remote_copy(
            src_ref=self.src(peer),
            dst_ref=self.dst.at[slot],
            send_sem=self.send_sem.at[d],
            recv_sem=self.recv_sem.at[d],
            device_id={"ep": peer},
            device_id_type=MESH,
        )

    def start(self):
        @pl.loop(1, self.n)
        def _(d):
            self.copy(d, self.me).start()

    def wait_recv(self):
        @pl.loop(1, self.n)
        def _(d):
            self.copy(d, lax.rem(self.me - d + self.n, self.n)).wait_recv()

    def wait_send(self):
        @pl.loop(1, self.n)
        def _(d):
            self.copy(d, self.me).wait_send()


def kernel(
    n, hpd, tok_ref, gain_ref, nkv_ref, len_ref, gain2_ref, ids_ref, score_ref,
    q_hbm, kv_hbm, gate_hbm, up_hbm, uv_hbm, out_hbm, down_hbm, eg_hbm, eu_hbm, ed_hbm,
    after_ref, layer_ref,
    q, kv, gate, up, uv, out, down, eg, eu, ed,
    row_f32, gain_rows, send1, recv1, ctx_send, ctx_recv, rs1_send, rs1_recv,
    send2, recv2, rs2_send, rs2_recv, wide, narrow, lhs, flat,
    load_sem, ssem, rsem,
):
    width = tok_ref.shape[1]
    chunks = width // (2 * W)
    half = width // 2
    me = lax.axis_index("ep")
    barrier = pltpu.get_barrier_semaphore()

    @pl.loop(1, n)
    def _(d):
        pl.semaphore_signal(
            barrier, inc=1, device_id={"ep": lax.rem(me + d, n)}, device_id_type=MESH
        )

    jobs = [(q_hbm, q, None), (kv_hbm, kv, None)]
    jobs += [(src, dst, hf) for hf in (0, 1) for src, dst in ((gate_hbm, gate), (up_hbm, up))]
    jobs += [(uv_hbm, uv, None)]
    jobs += [(src, dst, hf) for hf in (0, 1) for src, dst in ((out_hbm, out), (down_hbm, down))]
    jobs += [(eg_hbm, eg, None), (eu_hbm, eu, None), (ed_hbm, ed, None)]
    loads = []
    for i, (src, dst, hf) in enumerate(jobs):
        if hf is not None:
            src, dst = (ref.at[:, pl.ds(hf * half, half)] for ref in (src, dst))
        loads.append(pltpu.make_async_copy(src, dst, load_sem.at[i]))
        loads[-1].start()
    (q_in, kv_in, gate_a, up_a, gate_b, up_b, uv_in, out_a, down_a, out_b, down_b,
     eg_in, eu_in, ed_in) = loads
    projections = ((gate_a, up_a), (gate_b, up_b))
    branches = ((out_a, down_a), (out_b, down_b))

    def fold(src, dst):
        dst[...] = jnp.zeros_like(dst)
        for j in range(2 * chunks):
            hf, c = divmod(j, chunks)
            dst[c : c + 1, hf * W : (hf + 1) * W] = src[0:1, j * W : (j + 1) * W].astype(F32)

    def unfold(values, dst):
        for j in range(2 * chunks):
            hf, c = divmod(j, chunks)
            dst[0:1, j * W : (j + 1) * W] = values[c : c + 1, hf * W : (hf + 1) * W].astype(BF16)

    def norm(values, gain):
        squares = jnp.sum(jnp.sum(values * values, axis=1, keepdims=True), axis=0, keepdims=True)
        return values * lax.rsqrt(squares / width + 1e-06) * gain

    def unfold_rows(buffer):
        wide[...] = buffer[...].astype(F32)
        for j in range(2 * chunks):
            hf, c = divmod(j, chunks)
            lhs[j] = wide[:, c, hf * W : (hf + 1) * W].astype(BF16)

    def total(buffer, hf):
        def step(i, acc):
            return acc + buffer[hf, i].astype(F32)

        return lax.fori_loop(0, n, step, jnp.zeros((16, W), F32), unroll=4)

    def scatter(send, recv, hf, sem):
        send[hf] = narrow[...].astype(BF16)
        recv[hf, me] = send[hf, me]
        exchange = Exchange(
            n, me, lambda peer: send.at[hf, peer], recv.at[hf], ssem.at[sem], rsem.at[sem]
        )
        exchange.start()
        return exchange

    narrow[...] = jnp.zeros_like(narrow)
    rows = lax.broadcasted_iota(jnp.int32, (16, 2 * W), 0)
    lanes = lax.broadcasted_iota(jnp.int32, (16, 2 * W), 1)

    fold(tok_ref, row_f32)
    fold(gain_ref, gain_rows)
    send1[...] = norm(row_f32[...], gain_rows[...]).astype(BF16)
    gather1 = Exchange(n, me, lambda peer: send1, recv1, ssem.at[0], rsem.at[0])
    recv1[me] = send1[...]
    pl.semaphore_wait(barrier, n - 1)
    gather1.start()

    q_in.wait()
    kv_in.wait()
    factor = (HV + ROPE) ** (-0.5)
    queries = q[...].astype(F32).T
    scores = dot(queries.astype(BF16), kv[...]) * factor
    fresh = nkv_ref[...].astype(F32)
    own = jnp.sum(queries * fresh, axis=1, keepdims=True) * factor
    usable = lax.broadcasted_iota(jnp.int32, scores.shape, 1) < len_ref[...]
    highest = jnp.maximum(
        jnp.max(jnp.where(usable, scores, -jnp.inf), axis=1, keepdims=True), own
    )
    weights = jnp.where(usable, jnp.exp(scores - highest), 0.0)
    own_weight = jnp.exp(own - highest)
    totals = jnp.sum(weights, axis=1, keepdims=True) + own_weight
    probs = (weights / totals).astype(BF16)
    probs_own = (own_weight / totals).astype(BF16).astype(F32)
    context = dot_nt(probs, kv[:LAT, :]) + probs_own * fresh[:, :LAT]
    ctx_send[...] = context.astype(BF16).astype(F32).reshape(ctx_send.shape)
    ctx_recv[me] = ctx_send[me]
    spread = Exchange(n, me, lambda peer: ctx_send.at[peer], ctx_recv, ssem.at[1], rsem.at[1])
    spread.start()

    gather1.wait_recv()
    unfold_rows(recv1)
    gate_part = jnp.zeros((n, gate.shape[0]), F32)
    up_part = jnp.zeros((n, up.shape[0]), F32)
    for j in range(2 * chunks):
        if j % chunks == 0:
            for load in projections[j // chunks]:
                load.wait()
        part = slice(j * W, (j + 1) * W)
        gate_part += dot_nt(lhs[j], gate[:, part])
        up_part += dot_nt(lhs[j], up[:, part])
    hidden = (silu(gate_part) * up_part).astype(BF16)

    spread.wait_recv()
    uv_in.wait()
    for h in range(hpd):
        flat[:, h * HV : (h + 1) * HV] = dot(ctx_recv[:, h, :].astype(BF16), uv[h]).astype(BF16)
    heads = flat[...]
    sum1 = []
    for hf in (0, 1):
        for load in branches[hf]:
            load.wait()
        for c in range(chunks):
            part = slice(hf * half + c * W, hf * half + (c + 1) * W)
            narrow[:, c, :] = dot(hidden, down[:, part]) + dot(heads, out[:, part])
        sum1.append(scatter(rs1_send, rs1_recv, hf, 2 + hf))
    fold(gain2_ref, gain_rows)
    combine = (2.5 / ids_ref.shape[1] * score_ref[...]).astype(BF16).astype(F32)
    table = jnp.zeros((16, 2 * W), F32)
    for k in range(ids_ref.shape[1]):
        table += jnp.where(lanes == ids_ref[0:1, k : k + 1], combine[0:1, k : k + 1], 0.0)
    sums = []
    for hf in (0, 1):
        sum1[hf].wait_recv()
        sums.append(total(rs1_recv, hf))
    after = row_f32[...] + jnp.concatenate(sums, axis=1)
    after = jnp.where(rows < chunks, after, 0.0).astype(BF16).astype(F32)
    unfold(after, after_ref)
    row_f32[...] = after

    moe_in = norm(after, gain_rows[...])
    send2[...] = jnp.where(rows == chunks, table, moe_in).astype(BF16)
    recv2[me] = send2[...]
    gather2 = Exchange(n, me, lambda peer: send2, recv2, ssem.at[4], rsem.at[4])
    gather2.start()
    eg_in.wait()
    eu_in.wait()
    ed_in.wait()
    gather2.wait_recv()
    unfold_rows(recv2)
    columns = wide[:, chunks, :]
    mine = lax.broadcasted_iota(jnp.int32, columns.shape, 1) == me // GROUP
    column = jnp.sum(jnp.where(mine, columns, 0.0), axis=1, keepdims=True)
    gate_part = jnp.zeros((n, eg.shape[1]), F32)
    up_part = jnp.zeros((n, eu.shape[1]), F32)
    for j in range(2 * chunks):
        part = slice(j * W, (j + 1) * W)
        gate_part += dot(lhs[j], eg[part, :])
        up_part += dot(lhs[j], eu[part, :])
    expert_hidden = (silu(gate_part) * up_part).astype(BF16)
    sum2 = []
    for hf in (0, 1):
        for c in range(chunks):
            part = slice(hf * half + c * W, hf * half + (c + 1) * W)
            narrow[:, c, :] = dot(expert_hidden, ed[:, part]) * column
        sum2.append(scatter(rs2_send, rs2_recv, hf, 5 + hf))
    for exchange in (gather1, spread, *sum1, gather2):
        exchange.wait_send()
    sums = []
    for hf in (0, 1):
        sum2[hf].wait_recv()
        sums.append(total(rs2_recv, hf))
    layer = row_f32[...] + jnp.concatenate(sums, axis=1)
    unfold(layer, layer_ref)
    for exchange in sum2:
        exchange.wait_send()


def body(
    tokens, ffn_gain, gate_weight, up_weight, down_weight, queries, kv_cache, new_kv, lengths,
    uv_weight, out_weight, moe_gain, route_ids, route_scores, expert_gate, expert_up, expert_down,
):
    n = lax.axis_size("ep")
    width = tokens.shape[1]
    hpd = uv_weight.shape[0]
    chunks = width // (2 * W)
    assert tokens.shape[0] == 1 and width % (2 * W) == 0 and chunks < 16
    big = (
        queries[0].T, kv_cache[0].T, gate_weight.T, up_weight.T, uv_weight,
        out_weight.reshape(-1, width), down_weight,
        expert_gate[0], expert_up[0], expert_down[0],
    )
    vmem = pl.BlockSpec(memory_space=pltpu.VMEM)
    slots = pltpu.VMEM((n, 16, 2 * W), BF16)
    halves = pltpu.VMEM((2, n, 16, W), BF16)
    return pl.pallas_call(
        functools.partial(kernel, n, hpd),
        out_shape=[jax.ShapeDtypeStruct((1, width), BF16)] * 2,
        in_specs=[vmem] * 7 + [pl.BlockSpec(memory_space=pl.ANY)] * len(big),
        out_specs=[vmem] * 2,
        scratch_shapes=[pltpu.VMEM(x.shape, x.dtype) for x in big]
        + [
            pltpu.VMEM((16, 2 * W), F32),
            pltpu.VMEM((16, 2 * W), F32),
            pltpu.VMEM((16, 2 * W), BF16),
            slots,
            pltpu.VMEM((n, hpd, LAT), F32),
            pltpu.VMEM((n, hpd, LAT), F32),
            halves,
            halves,
            pltpu.VMEM((16, 2 * W), BF16),
            slots,
            halves,
            halves,
            pltpu.VMEM((n, 16, 2 * W), F32),
            pltpu.VMEM((n, 16, W), F32),
            pltpu.VMEM((2 * chunks, n, W), BF16),
            pltpu.VMEM((n, hpd * HV), BF16),
            pltpu.SemaphoreType.DMA((len(big) + 4,)),
            pltpu.SemaphoreType.DMA((7, n)),
            pltpu.SemaphoreType.DMA((7, n)),
        ],
        compiler_params=pltpu.CompilerParams(
            collective_id=0, has_side_effects=True, vmem_limit_bytes=60 * 1024 * 1024
        ),
    )(
        tokens, ffn_gain.reshape(1, width), new_kv, lengths.reshape(1, 1),
        moe_gain.reshape(1, width), route_ids, route_scores, *big,
    )


def solution(mesh):
    in_specs = (
        P(("rep", "ep"), None),
        P(),
        P(None, "ep"),
        P(None, "ep"),
        P("ep", None),
        P(("rep", "ep"), None, None),
        P(("rep", "ep"), None, None),
        P(("rep", "ep"), None),
        P(("rep", "ep")),
        P("ep", None, None),
        P("ep", None, None),
        P(),
        P(("rep", "ep"), None),
        P(("rep", "ep"), None),
        P("ep", None, None),
        P("ep", None, None),
        P("ep", None, None),
    )
    out_specs = (P(("rep", "ep"), None), P(("rep", "ep"), None))
    return jax.shard_map(body, mesh=mesh, in_specs=in_specs, out_specs=out_specs, check_vma=False)
```

time: 82.7 us -> 55.1 us (0.67); the launches traced: 81.3 us -> 54.7 us
  local copies, waits for them, and re-layouts: 31.7 us -> 2.77 us
  Pallas kernels: 47 us -> 49.4 us
    unnamed x6 -> x2, local copies, waits for them, and re-layouts: 31.7 us -> 2.77 us
    pallas_call x1, Pallas kernels: 47 us -> 49.4 us  [body(): pl.pallas_call(functools.partial(kernel, n, hpd), out_shape=[jax.ShapeDty...]
where the time goes in v2:
time: 55.1 us; the launch traced here: 54.7 us
  Pallas kernels  49.4 us (90%)
  local copies, waits for them, and re-layouts  2.77 us (5%)
  between operations  2.58 us (5%)
    pallas_call x1, Pallas kernels, body(): pl.pallas_call(functools.partial(kernel, n, hpd), out_shape=[jax.ShapeDty...  49.4 us
    unnamed x2, local copies, waits for them, and re-layouts  2.77 us

profile of v2, /device:TPU:0, one launch (start us, length us, event | category | flops | bytes accessed | tf_op | source)
XLA Modules:
  0.0 54.7 jit_solution(18241276267245269373)
XLA Ops:
  2.6 49.4 %shard_map.176 = (bf16[1,7168]{1,0:T(2,128)(2,1)}, bf16[1,7168]{1,0:T(2,128)(2,1)}) custom-call(bf16[1,7168]{1,0:T(2,128)(2,1)} %tok_ref.1, f32[1,7168]{1,0:T(1,128)} %bitcast.24, bf16[1,576]{1,0:T(2,128)(2,1)} %nkv_ref.1, s32[1,1]{1,0:T(1,128)} %bitcast.15.len_ref, f32[1,7168]{1,0:T(1,128)} %bitcast.25, s32[1,1]{1,0:T(1,128)S(6)} %copy.22.ids_ref, ...), custom_call_target="tpu_custom_call" | custom-call | tf_op jit(solution)/shard_map/pallas_call | solution.py:266
  52.0 1.4 %copy.24 = bf16[1,7168]{1,0:T(2,128)(2,1)} copy(bf16[1,7168]{1,0:T(2,128)(2,1)} %get-tuple-element.4) | data formatting | bytes 28672
  53.3 1.4 %copy.25 = bf16[1,7168]{1,0:T(2,128)(2,1)} copy(bf16[1,7168]{1,0:T(2,128)(2,1)} %get-tuple-element.5) | data formatting | bytes 28672

commit v3 on v2

--- a/solution.py
+++ b/solution.py
@@ -67,7 +67,7 @@
     after_ref, layer_ref,
     q, kv, gate, up, uv, out, down, eg, eu, ed,
     row_f32, gain_rows, send1, recv1, ctx_send, ctx_recv, rs1_send, rs1_recv,
-    send2, recv2, rs2_send, rs2_recv, wide, narrow, lhs, flat,
+    send2, recv2, rs2_send, rs2_recv, wide, lhs, flat,
     load_sem, ssem, rsem,
 ):
     width = tok_ref.shape[1]
@@ -119,22 +119,19 @@
             hf, c = divmod(j, chunks)
             lhs[j] = wide[:, c, hf * W : (hf + 1) * W].astype(BF16)
 
-    def total(buffer, hf):
+    def total(buffer):
         def step(i, acc):
-            return acc + buffer[hf, i].astype(F32)
-
-        return lax.fori_loop(0, n, step, jnp.zeros((16, W), F32), unroll=4)
-
-    def scatter(send, recv, hf, sem):
-        send[hf] = narrow[...].astype(BF16)
-        recv[hf, me] = send[hf, me]
-        exchange = Exchange(
-            n, me, lambda peer: send.at[hf, peer], recv.at[hf], ssem.at[sem], rsem.at[sem]
-        )
+            return acc + buffer[i].astype(F32)
+
+        return lax.fori_loop(0, n, step, jnp.zeros((16, 2 * W), F32), unroll=8)
+
+    def scatter(send, recv, sem):
+        send[...] = wide[...].astype(BF16)
+        recv[me] = send[me]
+        exchange = Exchange(n, me, lambda peer: send.at[peer], recv, ssem.at[sem], rsem.at[sem])
         exchange.start()
         return exchange
 
-    narrow[...] = jnp.zeros_like(narrow)
     rows = lax.broadcasted_iota(jnp.int32, (16, 2 * W), 0)
     lanes = lax.broadcasted_iota(jnp.int32, (16, 2 * W), 1)
 
@@ -186,24 +183,20 @@
     for h in range(hpd):
         flat[:, h * HV : (h + 1) * HV] = dot(ctx_recv[:, h, :].astype(BF16), uv[h]).astype(BF16)
     heads = flat[...]
-    sum1 = []
     for hf in (0, 1):
         for load in branches[hf]:
             load.wait()
         for c in range(chunks):
             part = slice(hf * half + c * W, hf * half + (c + 1) * W)
-            narrow[:, c, :] = dot(hidden, down[:, part]) + dot(heads, out[:, part])
-        sum1.append(scatter(rs1_send, rs1_recv, hf, 2 + hf))
+            wide[:, c, hf * W : (hf + 1) * W] = dot(hidden, down[:, part]) + dot(heads, out[:, part])
+    sum1 = scatter(rs1_send, rs1_recv, 2)
     fold(gain2_ref, gain_rows)
     combine = (2.5 / ids_ref.shape[1] * score_ref[...]).astype(BF16).astype(F32)
     table = jnp.zeros((16, 2 * W), F32)
     for k in range(ids_ref.shape[1]):
         table += jnp.where(lanes == ids_ref[0:1, k : k + 1], combine[0:1, k : k + 1], 0.0)
-    sums = []
-    for hf in (0, 1):
-        sum1[hf].wait_recv()
-        sums.append(total(rs1_recv, hf))
-    after = row_f32[...] + jnp.concatenate(sums, axis=1)
+    sum1.wait_recv()
+    after = row_f32[...] + total(rs1_recv)
     after = jnp.where(rows < chunks, after, 0.0).astype(BF16).astype(F32)
     unfold(after, after_ref)
     row_f32[...] = after
@@ -211,7 +204,7 @@
     moe_in = norm(after, gain_rows[...])
     send2[...] = jnp.where(rows == chunks, table, moe_in).astype(BF16)
     recv2[me] = send2[...]
-    gather2 = Exchange(n, me, lambda peer: send2, recv2, ssem.at[4], rsem.at[4])
+    gather2 = Exchange(n, me, lambda peer: send2, recv2, ssem.at[3], rsem.at[3])
     gather2.start()
     eg_in.wait()
     eu_in.wait()
@@ -228,22 +221,17 @@
         gate_part += dot(lhs[j], eg[part, :])
         up_part += dot(lhs[j], eu[part, :])
     expert_hidden = (silu(gate_part) * up_part).astype(BF16)
-    sum2 = []
     for hf in (0, 1):
         for c in range(chunks):
             part = slice(hf * half + c * W, hf * half + (c + 1) * W)
-            narrow[:, c, :] = dot(expert_hidden, ed[:, part]) * column
-        sum2.append(scatter(rs2_send, rs2_recv, hf, 5 + hf))
-    for exchange in (gather1, spread, *sum1, gather2):
+            wide[:, c, hf * W : (hf + 1) * W] = dot(expert_hidden, ed[:, part]) * column
+    sum2 = scatter(rs2_send, rs2_recv, 4)
+    for exchange in (gather1, spread, sum1, gather2):
         exchange.wait_send()
-    sums = []
-    for hf in (0, 1):
-        sum2[hf].wait_recv()
-        sums.append(total(rs2_recv, hf))
-    layer = row_f32[...] + jnp.concatenate(sums, axis=1)
+    sum2.wait_recv()
+    layer = row_f32[...] + total(rs2_recv)
     unfold(layer, layer_ref)
-    for exchange in sum2:
-        exchange.wait_send()
+    sum2.wait_send()
 
 
 def body(
@@ -262,7 +250,6 @@
     )
     vmem = pl.BlockSpec(memory_space=pltpu.VMEM)
     slots = pltpu.VMEM((n, 16, 2 * W), BF16)
-    halves = pltpu.VMEM((2, n, 16, W), BF16)
     return pl.pallas_call(
         functools.partial(kernel, n, hpd),
         out_shape=[jax.ShapeDtypeStruct((1, width), BF16)] * 2,
@@ -276,19 +263,18 @@
             slots,
             pltpu.VMEM((n, hpd, LAT), F32),
             pltpu.VMEM((n, hpd, LAT), F32),
-            halves,
-            halves,
+            slots,
+            slots,
             pltpu.VMEM((16, 2 * W), BF16),
             slots,
-            halves,
-            halves,
+            slots,
+            slots,
             pltpu.VMEM((n, 16, 2 * W), F32),
-            pltpu.VMEM((n, 16, W), F32),
             pltpu.VMEM((2 * chunks, n, W), BF16),
             pltpu.VMEM((n, hpd * HV), BF16),
             pltpu.SemaphoreType.DMA((len(big) + 4,)),
-            pltpu.SemaphoreType.DMA((7, n)),
-            pltpu.SemaphoreType.DMA((7, n)),
+            pltpu.SemaphoreType.DMA((5, n)),
+            pltpu.SemaphoreType.DMA((5, n)),
         ],
         compiler_params=pltpu.CompilerParams(
             collective_id=0, has_side_effects=True, vmem_limit_bytes=60 * 1024 * 1024

time: 55.1 us -> 54.4 us (0.987)
  Pallas kernels: 49.4 us -> 48.7 us
    pallas_call x1, Pallas kernels: 49.4 us -> 48.7 us  [body(): pl.pallas_call(functools.partial(kernel, n, hpd), out_shape=[jax.ShapeDty...]
where the time goes in v3:
time: 54.4 us; the launch traced here: 54 us
  Pallas kernels  48.7 us (90%)
  local copies, waits for them, and re-layouts  2.77 us (5%)
  between operations  2.58 us (5%)
    pallas_call x1, Pallas kernels, body(): pl.pallas_call(functools.partial(kernel, n, hpd), out_shape=[jax.ShapeDty...  48.7 us
    unnamed x2, local copies, waits for them, and re-layouts  2.77 us

profile of v3, /device:TPU:0, one launch (start us, length us, event | category | flops | bytes accessed | tf_op | source)
XLA Modules:
  0.0 54.0 jit_solution(8815010163616435099)
XLA Ops:
  2.6 48.7 %shard_map.176 = (bf16[1,7168]{1,0:T(2,128)(2,1)}, bf16[1,7168]{1,0:T(2,128)(2,1)}) custom-call(bf16[1,7168]{1,0:T(2,128)(2,1)} %tok_ref.1, f32[1,7168]{1,0:T(1,128)} %bitcast.24, bf16[1,576]{1,0:T(2,128)(2,1)} %nkv_ref.1, s32[1,1]{1,0:T(1,128)} %bitcast.15.len_ref, f32[1,7168]{1,0:T(1,128)} %bitcast.25, s32[1,1]{1,0:T(1,128)S(6)} %copy.22.ids_ref, ...), custom_call_target="tpu_custom_call" | custom-call | tf_op jit(solution)/shard_map/pallas_call | solution.py:253
  51.3 1.4 %copy.24 = bf16[1,7168]{1,0:T(2,128)(2,1)} copy(bf16[1,7168]{1,0:T(2,128)(2,1)} %get-tuple-element.4) | data formatting | bytes 28672
  52.6 1.4 %copy.25 = bf16[1,7168]{1,0:T(2,128)(2,1)} copy(bf16[1,7168]{1,0:T(2,128)(2,1)} %get-tuple-element.5) | data formatting | bytes 28672
